TPU v7x, 32 devices: a whole 2x2x4 slice. The times are simulated.
32 devices in a mesh: corridor: 8 (over z, x), group: 4 (over y, core).
Axes of the slice: x: 2, y: 2, z: 4, core: 2. Of those that a mesh axis runs over, the one named last changes fastest.
Arguments:
- features: bfloat16 [384, 64, 512], P(('corridor', 'group')), may hold values from -6 to 6
- voxel_mask: int32 [384, 512], P(('corridor', 'group')), may hold values from 0 to 1, as said below
- neighbours: int32 [384, 26], P(('corridor', 'group')), may hold values from -1 to 383, as said below
- weight_first: bfloat16 [27, 64, 64], replicated, may hold values from -0.15625 to 0.15625
- gain_first: float32 [64], replicated, may hold values from 0.25 to 1.75
- offset_first: float32 [64], replicated, may hold values from -3 to 3
- weight_second: bfloat16 [27, 128, 64], replicated, may hold values from -0.15625 to 0.15625
- gain_second: float32 [128], replicated, may hold values from 0.25 to 1.75
- offset_second: float32 [128], replicated, may hold values from -3 to 3
Outputs:
- segment_features: bfloat16 [384, 128, 512], P(('corridor', 'group'))
Inputs may be any that keep to these rules, and one draw needn't show every extreme that they name: `neighbours`: global slot of a device's slot s is (corridor index * 4 + group index) * 12 + s. Entry d names the brick displaced by the d-th of the 26 nonzero triples (dx slowest, lexicographic); its owner's corridor index differs by at most one from the brick's own, and differs only where dx is nonzero, by dx. Adjacency is symmetric. Empty slots have an all-zero mask and only -1 entries, and no entry names them. `voxel_mask`: every occupied brick is a slot named by the adjacency of its neighbours.
All inputs are finite; a program needn't handle non-finite values.
Results may differ from a plain program's by a relative error of at most 0.0051.
Values may be sent and summed in bfloat16 or wider, within the bound.
A program may use at most 320 MiB of HBM per device.

v0:
```python
import jax
import jax.numpy as jnp
from jax import lax
from jax.sharding import PartitionSpec as P

DIRECTIONS = [
    (a, b, c) for a in (-1, 0, 1) for b in (-1, 0, 1) for c in (-1, 0, 1) if (a, b, c) != (0, 0, 0)
]


def extended(block, sides, width):
    for axis, dim in sides:
        count = lax.axis_size(axis)
        forward = [(i, i + 1) for i in range(count - 1)]
        backward = [(target, source) for source, target in forward]
        low = lax.ppermute(
            lax.slice_in_dim(block, block.shape[dim] - width, None, axis=dim), axis, forward
        )
        high = lax.ppermute(lax.slice_in_dim(block, 0, width, axis=dim), axis, backward)
        block = jnp.concatenate([low, block, high], axis=dim)
    return block


def cell_range(step):
    if step < 0:
        return (7, 8, 0)
    if step == 0:
        return (0, 8, 1)
    return (0, 1, 9)


def face_index(step):
    if step[0] != 0:
        return 1 if step[0] < 0 else 0
    if step[1] != 0:
        return 3 if step[1] < 0 else 2
    return 5 if step[2] < 0 else 4


def share_faces(faces, blocks):
    width = faces.shape[2]
    across = jnp.concatenate([faces[:, 0], faces[:, 1]], axis=0)
    received = extended(across, (("corridor", 0),), 2 * blocks)
    bundle = jnp.concatenate(
        [
            faces.reshape(blocks * 6, width),
            received[blocks : 2 * blocks],
            received[4 * blocks : 5 * blocks],
        ],
        axis=0,
    )
    pooled = lax.all_gather(bundle, "group", axis=0, tiled=True)
    return pooled


def conv_layer(field, mask_f, rows, valid, weight):
    blocks, chans = (field.shape[0], field.shape[1])
    outs = weight.shape[1]
    cube = field.reshape(blocks, chans, 8, 8, 8)
    faces = jnp.stack(
        [
            cube[:, :, 0],
            cube[:, :, 7],
            cube[:, :, :, 0],
            cube[:, :, :, 7],
            cube[:, :, :, :, 0],
            cube[:, :, :, :, 7],
        ],
        axis=1,
    )
    faces = faces.reshape(blocks, 6, chans * 64)
    pooled = share_faces(faces, blocks)
    padded = jnp.zeros((blocks, chans, 10, 10, 10), jnp.bfloat16)
    padded = padded.at[:, :, 1:9, 1:9, 1:9].set(cube)
    for idx, step in enumerate(DIRECTIONS):
        fetched = jnp.take(pooled, rows[:, idx], axis=0).reshape(blocks, chans, 8, 8)
        fetched = jnp.where(
            valid[:, idx][:, None, None, None], fetched, jnp.zeros((), jnp.bfloat16)
        )
        rx, ry, rz = (cell_range(step[0]), cell_range(step[1]), cell_range(step[2]))
        if step[0] != 0:
            piece = fetched[:, :, ry[0] : ry[1], rz[0] : rz[1]][:, :, None]
        elif step[1] != 0:
            piece = fetched[:, :, rx[0] : rx[1], rz[0] : rz[1]][:, :, :, None]
        else:
            piece = fetched[:, :, :, :, None]
        padded = padded.at[
            :,
            :,
            rx[2] : rx[2] + rx[1] - rx[0],
            ry[2] : ry[2] + ry[1] - ry[0],
            rz[2] : rz[2] + rz[1] - rz[0],
        ].set(piece)
    total = jnp.zeros((blocks, outs, 8, 8, 8), jnp.float32)
    for tap in range(27):
        oa, oe, of_ = (tap // 9, tap // 3 % 3, tap % 3)
        total = total + jnp.einsum(
            "oc,bcxyz->boxyz",
            weight[tap],
            padded[:, :, oa : oa + 8, oe : oe + 8, of_ : of_ + 8],
            preferred_element_type=jnp.float32,
        )
    return total.reshape(blocks, outs, 512) * mask_f[:, None, :]


def normalize(values, mask_f, gain, offset):
    local_sum = jnp.sum(values, axis=(0, 2))
    local_count = jnp.sum(mask_f)
    count, summed = lax.psum((local_count, local_sum), ("corridor", "group"))
    mean = summed / count
    deviation = values - mean[None, :, None]
    local_square = jnp.sum(mask_f[:, None, :] * deviation * deviation, axis=(0, 2))
    var = lax.psum(local_square, ("corridor", "group")) / count
    scaled = (
        gain[None, :, None] * deviation / jnp.sqrt(var[None, :, None] + 1e-05)
        + offset[None, :, None]
    )
    return (jnp.maximum(scaled, 0.0) * mask_f[:, None, :]).astype(jnp.bfloat16)


def shards(
    features,
    voxel_mask,
    neighbours,
    weight_first,
    gain_first,
    offset_first,
    weight_second,
    gain_second,
    offset_second,
):
    blocks = features.shape[0]
    lanes = lax.axis_size("group")
    corridor_at = lax.axis_index("corridor")
    mask_f = voxel_mask.astype(jnp.float32)
    masked = features * voxel_mask.astype(jnp.bfloat16)[:, None, :]
    valid = neighbours >= 0
    safe = jnp.maximum(neighbours, 0)
    owner = safe // blocks
    slot_in = safe % blocks
    section = owner // lanes - corridor_at + 1
    lane_of = owner % lanes
    face_pick = jnp.array([face_index(step) for step in DIRECTIONS], jnp.int32)
    lane_base = lane_of * (8 * blocks)
    own_row = lane_base + slot_in * 6 + face_pick[None, :]
    far_row = lane_base + jnp.where(section == 0, 6, 7) * blocks + slot_in
    location = jnp.where(section == 1, own_row, far_row)
    rows = jnp.where(valid, location, 0)
    first = conv_layer(masked, mask_f, rows, valid, weight_first)
    hidden = normalize(first, mask_f, gain_first, offset_first)
    second = conv_layer(hidden, mask_f, rows, valid, weight_second)
    return normalize(second, mask_f, gain_second, offset_second)


def solution(mesh):
    in_specs = (
        P(("corridor", "group"), None, None),
        P(("corridor", "group"), None),
        P(("corridor", "group"), None),
        P(),
        P(),
        P(),
        P(),
        P(),
        P(),
    )
    out_specs = P(("corridor", "group"), None, None)
    return jax.shard_map(shards, mesh=mesh, in_specs=in_specs, out_specs=out_specs, check_vma=False)
```

profile of v0, /device:TPU:0, one launch (start us, length us, event | category | flops | bytes accessed | tf_op | source)
XLA Modules:
  0.0 1103.8 jit_solution(5214209502823967963)
XLA Ops:
  12.5 3.9 squeeze.278
  18.3 3.9 squeeze.279
  22.2 4.9 collective-permute-start
  33.6 12.3 %copy.67 = bf16[12,6,64,8,8]{4,3,2,1,0:T(8,128)(2,1)} copy(bf16[12,6,64,8,8]{2,0,4,3,1:T(8,128)(2,1)} %fusion.60) | data formatting | bytes 1179648 | tf_op jit(solution)/shard_map/stack | solution.py:60
  45.8 14.3 %reshape_reshape.6 = bf16[72,4096]{1,0:T(8,128)(2,1)S(1)} reshape(bf16[12,6,64,8,8]{4,3,2,1,0:T(8,128)(2,1)} %copy.67) | data formatting | bytes 1179648 | tf_op jit(solution)/shard_map/reshape;reshape | solution.py:46
  88.1 12.7 %all-gather.3.cloned.1.call-done = bf16[384,4096]{1,0:T(8,128)(2,1)} async-done(((bf16[96,4096]{1,0:T(8,128)(2,1)}), bf16[384,4096]{1,0:T(8,128)(2,1)}) %all-gather.3.cloned.1.call-update) | async-done | bytes 3145744 | tf_op jit(solution)/shard_map/all_gather | solution.py:52
  159.4 3.9 copy.237
  272.9 3.9 reshape.2779
  390.2 4.4 fusion.100
  461.3 36.8 %fusion.208 = (f32[64]{0:T(128)S(1)}, f32[12,64,8,8,8]{1,0,4,3,2:T(8,128)}) fusion(f32[12,8,8,8]{0,3,2,1:T(8,128)S(1)} %copy.104, bf16[12,64,10,10,10]{1,0,4,3,2:T(8,128)(2,1)} %constant_dynamic-update-slice_fusion.8, bf16[27,64,64]{2,1,0:T(8,128)(2,1)S(1)} %copy-done.37, f32[12,8,8,8,64]{4,0,3,2,1:T(8,128)} %fusion.92, f32[12,8,8,8,64]{4,0,3,2,1:T(8,128)} %fusion.94, ...), kind=kOutput, calls=%fused_computation.552 | convolution fusion | flops 61341632 | bytes 44282112 | tf_op jit(solution)/shard_map/oc,bcxyz->boxyz/dot_general | solution.py:97
  498.0 39.6 %all-reduce.2 = (f32[64]{0:T(128)S(1)}, f32[]{:T(128)}) all-reduce(f32[64]{0:T(128)S(1)} %get-tuple-element.741, f32[]{:T(128)} %convert_reduce_fusion), channel_id=1, replica_groups=mesh['corridor'=8,'group'=4] {'corridor','group'}, use_global_device_ids=true, to_apply=%region_1.3 | all-reduce | flops 65 | bytes 520 | tf_op jit(solution)/shard_map/psum | solution.py:109
  541.2 41.3 %psum.40 = f32[64]{0:T(128)S(1)} all-reduce(f32[64]{0:T(128)S(1)} %fusion), channel_id=1, replica_groups=mesh['corridor'=8,'group'=4] {'corridor','group'}, use_global_device_ids=true, to_apply=%region_5.7 | all-reduce | flops 64 | bytes 512 | tf_op jit(solution)/shard_map/psum | solution.py:113
  588.7 3.9 squeeze.333
  594.4 3.9 squeeze.334
  598.3 4.2 collective-permute-start.2
  607.6 12.6 %copy.108 = bf16[12,6,64,8,8]{4,3,2,1,0:T(8,128)(2,1)} copy(bf16[12,6,64,8,8]{2,0,4,3,1:T(8,128)(2,1)} %fusion.56) | data formatting | bytes 1179648 | tf_op jit(solution)/shard_map/stack | solution.py:60
  620.2 14.3 %reshape_reshape.7 = bf16[72,4096]{1,0:T(8,128)(2,1)S(1)} reshape(bf16[12,6,64,8,8]{4,3,2,1,0:T(8,128)(2,1)} %copy.108) | data formatting | bytes 1179648 | tf_op jit(solution)/shard_map/reshape;reshape | solution.py:46
  638.4 26.9 %all-gather.5.cloned.1.call-done = bf16[384,4096]{1,0:T(8,128)(2,1)} async-done(((bf16[96,4096]{1,0:T(8,128)(2,1)}), bf16[384,4096]{1,0:T(8,128)(2,1)}) %all-gather.5.cloned.1.call-update) | async-done | bytes 3145744 | tf_op jit(solution)/shard_map/all_gather | solution.py:52
  891.3 27.9 %fusion.203 = (bf16[12,64,8,8,8]{1,0,4,3,2:T(8,128)(2,1)}, bf16[12,64,8,8,8]{1,0,4,3,2:T(8,128)(2,1)}, bf16[12,64,8,8,8]{1,0,4,3,2:T(8,128)(2,1)}, bf16[12,64,8,...) fusion(bf16[12,64,10,10,10]{1,0,4,3,2:T(8,128)(2,1)} %constant_, ...), kind=kLoop, calls=%fused_computation.547 | loop fusion | bytes 29884416 | tf_op jit(solution)/shard_map/slice | solution.py:100
  919.2 5.3 fusion.204
  982.6 24.9 %multiply_reduce_fusion = (f32[128]{0:T(128)S(1)}, f32[12,128,8,8,8]{1,4,3,2,0:T(8,128)S(1)}) fusion(f32[12,8,8,8]{3,2,1,0:T(8,128)S(1)} %copy-done.26, f32[12,8,8,8,128]{4,3,2,1,0:T(8,128)} %fusion.3, f32[12,8,8,8,128]{4,3,2,1,0:T(8,128)} %fusion.5, f32[12,8,8,8,128]{4,3,2,1,0:T(8,128)} %fusion.7, f32[12,8,8,8,128]{4,3,2,1,0:T(8,128)} %fusion.9, ...), kind=kOutput, calls=%fused_computation.79 | convolution fusion | flops 122683264 | bytes 87073280 | tf_op jit(solution)/shard_map/oc,bcxyz->boxyz/dot_general | solution.py:97
  1007.5 39.4 %psum.41 = f32[128]{0:T(128)S(1)} all-reduce(f32[128]{0:T(128)S(1)} %get-tuple-element.743), channel_id=1, replica_groups=mesh['corridor'=8,'group'=4] {'corridor','group'}, use_global_device_ids=true, to_apply=%region_7.9 | all-reduce | flops 128 | bytes 1024 | tf_op jit(solution)/shard_map/psum | solution.py:109
  1048.5 41.0 %psum.42 = f32[128]{0:T(128)S(1)} all-reduce(f32[128]{0:T(128)S(1)} %fusion.2), channel_id=1, replica_groups=mesh['corridor'=8,'group'=4] {'corridor','group'}, use_global_device_ids=true, to_apply=%region_9.11 | all-reduce | flops 128 | bytes 1024 | tf_op jit(solution)/shard_map/psum | solution.py:113
  1092.6 3.9 multiply_convert_fusion.1
  (651 shorter events, 698.2 us)
Async XLA Ops:
  6.5 94.3 %all-gather.3.cloned.1.call-start = ((), (), s32[]{:S(2)}) async-start(), calls=%async_computation | async-start | bytes 3932160 | tf_op jit(solution)/shard_map/all_gather | solution.py:52
  7.4 65.7 %copy-start.39 = (f32[12,512]{1,0:T(8,128)}, f32[12,512]{1,0:T(8,128)S(1)}, u32[]{:S(2)}) copy-start(f32[12,512]{1,0:T(8,128)S(1)} %get-tuple-element.739) | copy-start | bytes 73732
  22.2 46.4 %collective-permute-start = (bf16[24,4096]{1,0:T(8,128)(2,1)S(1)}, bf16[24,4096]{1,0:T(8,128)(2,1)S(1)}, u32[]{:S(2)}, u32[]{:S(2)}) collective-permute-start(bf16[24,4096]{1,0:T(8,128)(2,1)S(1)} %pad_maximum_fusion.2), channel_id=1, source_target_pairs={{0,4},{4,8},{8,12},{12,16},{16,20},{20,24},{24,28},{1,5},{5,9},{9,... | collective-permute-start | bytes 589832 | tf_op jit(solution)/shard_map/ppermute | solution.py:16
  27.1 41.6 %collective-permute-start.1 = (bf16[24,4096]{1,0:T(8,128)(2,1)S(1)}, bf16[24,4096]{1,0:T(8,128)(2,1)S(1)}, u32[]{:S(2)}, u32[]{:S(2)}) collective-permute-start(bf16[24,4096]{1,0:T(8,128)(2,1)S(1)} %pad_maximum_fusion.2), channel_id=1, source_target_pairs={{4,0},{8,4},{12,8},{16,12},{20,16},{24,20},{28,24},{5,1},{9,5},{13... | collective-permute-start | bytes 589832 | tf_op jit(solution)/shard_map/ppermute | solution.py:19
  60.2 40.6 %copy-start.65 = (s32[1024]{0:T(1024)}, s32[1024]{0:T(1024)S(1)}, u32[]{:S(2)}) copy-start(s32[1024]{0:T(1024)S(1)} %pad_clamp_fusion.25) | copy-start | bytes 12292
  60.8 62.4 %copy-start.64 = (s32[1024]{0:T(1024)}, s32[1024]{0:T(1024)S(1)}, u32[]{:S(2)}) copy-start(s32[1024]{0:T(1024)S(1)} %pad_clamp_fusion.23) | copy-start | bytes 12292
  62.6 100.7 %copy-start.63 = (s32[1024]{0:T(1024)}, s32[1024]{0:T(1024)S(1)}, u32[]{:S(2)}) copy-start(s32[1024]{0:T(1024)S(1)} %pad_clamp_fusion.19) | copy-start | bytes 12292
  63.2 119.4 %copy-start.62 = (s32[1024]{0:T(1024)}, s32[1024]{0:T(1024)S(1)}, u32[]{:S(2)}) copy-start(s32[1024]{0:T(1024)S(1)} %pad_clamp_fusion.17) | copy-start | bytes 12292
  69.7 595.6 %all-gather.5.cloned.1.call-start = ((), (), s32[]{:S(2)}) async-start(), calls=%async_computation.1 | async-start | bytes 3932160 | tf_op jit(solution)/shard_map/all_gather | solution.py:52
  355.6 28.2 %copy-start.52 = (bf16[12,64,8,1]{1,0,3,2:T(8,128)(2,1)S(1)}, bf16[12,64,8,1]{1,0,3,2:T(8,128)(2,1)}, u32[]{:S(2)}) copy-start(bf16[12,64,8,1]{1,0,3,2:T(8,128)(2,1)} %copy.248) | copy-start | bytes 36868
  355.6 28.2 %copy-start.69 = (pred[12]{0:T(512)(128)(4,1)S(1)}, pred[12]{0:T(512)(128)(4,1)}, u32[]{:S(2)}) copy-start(pred[12]{0:T(512)(128)(4,1)} %get-tuple-element.685) | copy-start | bytes 40
  355.6 28.9 %copy-start.68 = (pred[12]{0:T(512)(128)(4,1)S(1)}, pred[12]{0:T(512)(128)(4,1)}, u32[]{:S(2)}) copy-start(pred[12]{0:T(512)(128)(4,1)} %get-tuple-element.684) | copy-start | bytes 40
  355.6 30.6 %copy-start.53 = (bf16[12,64,8,1]{1,0,3,2:T(8,128)(2,1)S(1)}, bf16[12,64,8,1]{1,0,3,2:T(8,128)(2,1)}, u32[]{:S(2)}) copy-start(bf16[12,64,8,1]{1,0,3,2:T(8,128)(2,1)} %copy.249) | copy-start | bytes 36868
  355.6 30.6 %copy-start.67 = (pred[12]{0:T(512)(128)(4,1)S(1)}, pred[12]{0:T(512)(128)(4,1)}, u32[]{:S(2)}) copy-start(pred[12]{0:T(512)(128)(4,1)} %get-tuple-element.683) | copy-start | bytes 40
  355.6 31.3 %copy-start.61 = (bf16[12,64,1,1]{1,0,3,2:T(8,128)(2,1)S(1)}, bf16[12,64,1,1]{1,0,3,2:T(8,128)(2,1)}, u32[]{:S(2)}) copy-start(bf16[12,64,1,1]{1,0,3,2:T(8,128)(2,1)} %copy.250) | copy-start | bytes 4612
  355.6 32.6 %copy-start.56 = (bf16[12,64,1,8]{1,0,3,2:T(8,128)(2,1)S(1)}, bf16[12,64,1,8]{1,0,3,2:T(8,128)(2,1)}, u32[]{:S(2)}) copy-start(bf16[12,64,1,8]{1,0,3,2:T(8,128)(2,1)} %copy.251) | copy-start | bytes 36868
  355.6 32.6 %copy-start.66 = (pred[12]{0:T(512)(128)(4,1)S(1)}, pred[12]{0:T(512)(128)(4,1)}, u32[]{:S(2)}) copy-start(pred[12]{0:T(512)(128)(4,1)} %get-tuple-element.681) | copy-start | bytes 40
  498.0 85.1 %copy-start.95 = (f32[64]{0:T(128)S(1)}, f32[64]{0:T(128)}, u32[]{:S(2)}) copy-start(f32[64]{0:T(128)} %param.125) | copy-start | bytes 772
  498.0 85.1 %copy-start.96 = (f32[64]{0:T(128)S(1)}, f32[64]{0:T(128)}, u32[]{:S(2)}) copy-start(f32[64]{0:T(128)} %param.124) | copy-start | bytes 772
  598.3 36.1 %collective-permute-start.2 = (bf16[24,4096]{1,0:T(8,128)(2,1)S(1)}, bf16[24,4096]{1,0:T(8,128)(2,1)S(1)}, u32[]{:S(2)}, u32[]{:S(2)}) collective-permute-start(bf16[24,4096]{1,0:T(8,128)(2,1)S(1)} %pad_maximum_fusion.3), channel_id=1, source_target_pairs={{0,4},{4,8},{8,12},{12,16},{16,20},{20,24},{24,28},{1,5},{5,9},{9,... | collective-permute-start | bytes 589832 | tf_op jit(solution)/shard_map/ppermute | solution.py:16
  602.5 32.0 %collective-permute-start.3 = (bf16[24,4096]{1,0:T(8,128)(2,1)S(1)}, bf16[24,4096]{1,0:T(8,128)(2,1)S(1)}, u32[]{:S(2)}, u32[]{:S(2)}) collective-permute-start(bf16[24,4096]{1,0:T(8,128)(2,1)S(1)} %pad_maximum_fusion.3), channel_id=1, source_target_pairs={{4,0},{8,4},{12,8},{16,12},{20,16},{24,20},{28,24},{5,1},{9,5},{13... | collective-permute-start | bytes 589832 | tf_op jit(solution)/shard_map/ppermute | solution.py:19
  635.6 33.0 %copy-start.92 = (pred[12]{0:T(512)(128)(4,1)S(1)}, pred[12]{0:T(512)(128)(4,1)}, u32[]{:S(2)}) copy-start(pred[12]{0:T(512)(128)(4,1)} %get-tuple-element.796) | copy-start | bytes 40
  638.4 36.4 %copy-start.91 = (pred[12]{0:T(512)(128)(4,1)S(1)}, pred[12]{0:T(512)(128)(4,1)}, u32[]{:S(2)}) copy-start(pred[12]{0:T(512)(128)(4,1)} %get-tuple-element.795) | copy-start | bytes 40
  857.5 28.3 %copy-start.51 = (bf16[12,64,8,1]{1,0,3,2:T(8,128)(2,1)S(1)}, bf16[12,64,8,1]{1,0,3,2:T(8,128)(2,1)}, u32[]{:S(2)}) copy-start(bf16[12,64,8,1]{1,0,3,2:T(8,128)(2,1)} %copy.269) | copy-start | bytes 36868
  (82 other events, 916.4 us)
Sparse Core Ops, SparseCore 0:
  69.8 30.9 all-gather.2
  635.7 29.5 all-gather.4
where the time goes:
time: 1120 us; the launch traced here: 1100 us
  local copies, waits for them, and re-layouts  540 us (48%)
  matrix products  189 us (17%)
  blocking collectives  161 us (14%)
  other arithmetic  146 us (13%)
  waiting for transfers between devices  39.7 us (4%)
  between operations  15.7 us (1%)
  starting transfers between devices  11.7 us (1%)
    reshape x64, local copies, waits for them, and re-layouts, conv_layer(): jnp.take(pooled, rows[:, idx], axis=0).reshape(blocks, chans, 8, 8)  203 us
    dot_general x54, matrix products, conv_layer(): jnp.einsum('oc,bcxyz->boxyz', weight[tap], padded[:, :, oa:oa + 8, oe:oe...  189 us
    unnamed x250, local copies, waits for them, and re-layouts  94.5 us
    psum x2, blocking collectives, normalize(): var = lax.psum(local_square, ('corridor', 'group')) / count  82.3 us
    psum x2, blocking collectives, normalize(): count, summed = lax.psum((local_count, local_sum), ('corridor', 'group'))  79 us
    scatter x52, other arithmetic, conv_layer(): padded = padded.at[:, :, rx[2]:rx[2] + rx[1] - rx[0], ry[2]:ry[2] + ry[1]...  66.2 us
    slice x28, local copies, waits for them, and re-layouts, conv_layer(): piece = fetched[:, :, ry[0]:ry[1], rz[0]:rz[1]][:, :, None]  61.7 us
    gather x52, local copies, waits for them, and re-layouts, conv_layer(): jnp.take(pooled, rows[:, idx], axis=0).reshape(blocks, chans, 8, 8)  43.6 us
  transfers between devices with their start and end apart: 6, of which 2 were waited for; matrix products, arithmetic and copies ran while one was open for 8% of the time, Pallas kernels for 0%

commit v1 on v0

v1 whole, which is shorter than its diff:
```python
import functools

import jax
import jax.numpy as jnp
from jax import lax
from jax.experimental import pallas as pl
from jax.experimental.pallas import tpu as pltpu
from jax.sharding import PartitionSpec as P

DIRECTIONS = [
    (a, b, c) for a in (-1, 0, 1) for b in (-1, 0, 1) for c in (-1, 0, 1) if (a, b, c) != (0, 0, 0)
]
AT = {step: idx for idx, step in enumerate(DIRECTIONS)}
SOURCES = ((0, 1, 2, 3, 4, 5, 8, -1), (2, 3, 4, 5, 8, -1, 6, 7))
F32 = jnp.float32
BF16 = jnp.bfloat16
VMEM = pl.BlockSpec(memory_space=pltpu.VMEM)
SMEM = pl.BlockSpec(memory_space=pltpu.SMEM)
MESH = pl.DeviceIdType.MESH


def params(mib, **kw):
    return pltpu.CompilerParams(vmem_limit_bytes=mib * 1024 * 1024, **kw)


def spread(mask_rows, width):
    shift = {64: 6, 128: 7}[width]
    row = lax.broadcasted_iota(jnp.int32, (128, 8 * width), 0)
    lane = lax.broadcasted_iota(jnp.int32, (128, 8 * width), 1)
    pick = jnp.where((lane >> shift) == row, 1.0, 0.0).astype(BF16)
    return jnp.dot(mask_rows, pick, preferred_element_type=F32)


def emit_field(nb, tiles, field_ref, bundle_ref, z_ref):
    face = nb * 8
    for t in range(4):
        value = tiles[t]
        cols = slice(128 * t, 128 * t + 128)
        field_ref[:, cols] = value[...].astype(BF16)
        bundle_ref[0:face, cols] = value[0:face, :].astype(BF16)
        bundle_ref[face : 2 * face, cols] = value[7 * face : 8 * face, :].astype(BF16)
        bundle_ref[2 * face : 3 * face, cols] = value[pl.ds(0, face, stride=8), :].astype(BF16)
        bundle_ref[3 * face : 4 * face, cols] = value[pl.ds(7, face, stride=8), :].astype(BF16)
    lane = lax.broadcasted_iota(jnp.int32, (8 * face, 128), 1)
    z_ref[...] = jnp.where(lane < 64, tiles[0][...], tiles[3][...]).astype(BF16)


def field_shapes(nb):
    return (
        jax.ShapeDtypeStruct((nb * 64, 512), BF16),
        jax.ShapeDtypeStruct((nb * 32, 512), BF16),
        jax.ShapeDtypeStruct((nb * 64, 128), BF16),
    )


def prepare_kernel(nb, x_ref, m_ref, field_ref, bundle_ref, z_ref, t_ref, *tiles):
    lane = lax.broadcasted_iota(jnp.int32, (64, 128), 1)
    for pair in range(nb // 2):
        halves = [
            x_ref[2 * pair + k].astype(F32) * m_ref[pl.ds(2 * pair + k, 1), :] for k in range(2)
        ]
        t_ref[...] = jnp.concatenate(halves, axis=0).T
        for t in range(4):
            even = t_ref[pl.ds(2 * t, 64, stride=8), :]
            odd = t_ref[pl.ds(2 * t + 1, 64, stride=8), :]
            first = jnp.where(lane < 64, even, pltpu.roll(odd, 64, 1))
            second = jnp.where(lane < 64, pltpu.roll(even, 64, 1), odd)
            for x in range(8):
                base = x * nb * 8 + pair * 16
                tiles[t][base : base + 8, :] = first[8 * x : 8 * x + 8]
                tiles[t][base + 8 : base + 16, :] = second[8 * x : 8 * x + 8]
    emit_field(nb, tiles, field_ref, bundle_ref, z_ref)


def prepare(features, mask_f):
    nb = features.shape[0]
    return pl.pallas_call(
        functools.partial(prepare_kernel, nb),
        out_shape=field_shapes(nb),
        in_specs=[VMEM, VMEM],
        out_specs=(VMEM, VMEM, VMEM),
        scratch_shapes=[pltpu.VMEM((512, 128), F32)]
        + [pltpu.VMEM((nb * 64, 128), F32) for _ in range(4)],
        compiler_params=params(32),
    )(features, mask_f)


def conv_kernel(
    nb, lanes, outs, rows_ref, field_ref, pool_ref, zpool_ref, w_ref, m_ref,
    out_ref, stat_ref, own_ref, pf_ref, zf_ref, q_ref, wb_ref,
):
    face = nb * 8
    total = pool_ref.shape[0]
    ztotal = zpool_ref.shape[0]
    own_ref[...] = field_ref[...].astype(F32)
    pf_ref[0:total, :] = pool_ref[...].astype(F32)
    pf_ref[total:, :] = jnp.zeros((face, 512), F32)
    zf_ref[0:ztotal, :] = zpool_ref[...].astype(F32)
    zf_ref[ztotal:, :] = jnp.zeros((8 * face, 128), F32)

    wb_ref[...] = jnp.zeros(wb_ref.shape, BF16)
    for half in range(2):
        for a in range(3):
            for e in range(3):
                for at, source in enumerate(SOURCES[half]):
                    row = e * 512 + at * 64
                    for q in range(outs * 4 // 128):
                        z = 4 * half + q * 128 // outs
                        f = source - z + 1
                        kinds = 3 if outs == 128 else 4
                        if 0 <= f < kinds:
                            block = ((a * 3 + e) * kinds + f) * 64
                            wb_ref[half, a, row : row + 64, q * 128 : q * 128 + 128] = w_ref[
                                block : block + 64, :
                            ]

    low = lax.broadcasted_iota(jnp.int32, (8, 128), 1) < 64
    sub = lax.broadcasted_iota(jnp.int32, (8, 128), 0)

    def brick_planes(b):
        def at(dx, dy, dz):
            return rows_ref[b, AT[(dx, dy, dz)]]

        def faces(load):
            main = load(0)
            up = load(1)
            down = load(-1)
            tiles = [main[:, 128 * t : 128 * t + 128] for t in range(4)]
            width = main.shape[0]
            halo = jnp.where(low[:width], up[:, 0:128], down[:, 384:512])
            return [tiles[0], tiles[1], tiles[2], halo, tiles[3]]

        def x_face(dx, dy):
            def load(dz):
                return pf_ref[pl.ds(pl.multiple_of(at(dx, dy, dz), 8), 8), :]

            return faces(load)

        def y_row(dy, x):
            def load(dz):
                return pf_ref[pl.ds(at(0, dy, dz) + x * nb, 1), :]

            return [jnp.broadcast_to(v, (8, 128)) for v in faces(load)]

        def inner(x):
            base = pl.multiple_of(x * face + b * 8, 8)
            own = own_ref[pl.ds(base, 8), :]
            up = zf_ref[pl.ds(pl.multiple_of(at(0, 0, 1) + x * face, 8), 8), :]
            down = zf_ref[pl.ds(pl.multiple_of(at(0, 0, -1) + x * face, 8), 8), :]
            tiles = [own[:, 128 * t : 128 * t + 128] for t in range(4)]
            return [tiles[0], tiles[1], tiles[2], jnp.where(low, up, down), tiles[3]]

        planes = []
        for i in range(10):
            if i == 0 or i == 9:
                dx = -1 if i == 0 else 1
                centre = x_face(dx, 0)
                before = x_face(dx, -1)
                after = x_face(dx, 1)
            else:
                centre = inner(i - 1)
                before = y_row(-1, i - 1)
                after = y_row(1, i - 1)
            shifted0 = [
                pltpu.roll(jnp.where(sub == 7, n, c), 1, 0) for n, c in zip(before, centre)
            ]
            shifted2 = [
                pltpu.roll(jnp.where(sub == 0, n, c), 7, 0) for n, c in zip(after, centre)
            ]
            planes.append((shifted0, centre, shifted2))
        return planes

    @pl.loop(0, nb // 2)
    def _(pair):
        first = brick_planes(2 * pair)
        second = brick_planes(2 * pair + 1)
        for i in range(10):
            rows = pl.ds(pl.multiple_of(i * face + pair * 16, 16), 16)
            for e in range(3):
                tiles = [
                    jnp.concatenate([u, v], axis=0).astype(BF16)
                    for u, v in zip(first[i][e], second[i][e])
                ]
                for t in range(4):
                    q_ref[0, rows, e * 512 + t * 128 : e * 512 + t * 128 + 128] = tiles[t]
                    q_ref[1, rows, e * 512 + t * 128 : e * 512 + t * 128 + 128] = tiles[t + 1]

    mask_rows = m_ref[...]
    mask = spread(mask_rows, outs)
    sums = jnp.zeros((1, 128), F32)
    for half in range(2):
        acc = None
        for a in range(3):
            part = jnp.dot(
                q_ref[half, a * face : a * face + 8 * face, :],
                wb_ref[half, a],
                preferred_element_type=F32,
            )
            acc = part if acc is None else acc + part
        span = slice(half * 4 * outs, half * 4 * outs + 4 * outs)
        acc = acc * mask[:, span]
        out_ref[:, span] = acc
        column = jnp.sum(acc, axis=0, keepdims=True)
        for t in range(4 * outs // 128):
            sums = sums + column[:, 128 * t : 128 * t + 128]
    if outs == 64:
        sums = sums + pltpu.roll(sums, 64, 1)
    count = jnp.sum(mask_rows.astype(F32))
    mean = sums / jnp.maximum(count, 1.0)
    squares = jnp.zeros((1, 128), F32)
    for t in range(8 * outs // 128):
        span = slice(128 * t, 128 * t + 128)
        deviation = (out_ref[:, span] - mean) * mask[:, span]
        squares = squares + jnp.sum(deviation * deviation, axis=0, keepdims=True)
    if outs == 64:
        squares = squares + pltpu.roll(squares, 64, 1)
    stat_ref[...] = jnp.zeros((8, 128), F32)
    stat_ref[0:1, :] = sums
    stat_ref[1:2, :] = squares
    stat_ref[2:3, :] = jnp.full((1, 128), count, F32)


def conv(rows, field, pool, zpool, weight, mask_rows, lanes, outs):
    nb = rows.shape[0]
    return pl.pallas_call(
        functools.partial(conv_kernel, nb, lanes, outs),
        out_shape=(
            jax.ShapeDtypeStruct((nb * 64, 8 * outs), F32),
            jax.ShapeDtypeStruct((8, 128), F32),
        ),
        in_specs=[SMEM, VMEM, VMEM, VMEM, VMEM, VMEM],
        out_specs=(VMEM, VMEM),
        scratch_shapes=[
            pltpu.VMEM((nb * 64, 512), F32),
            pltpu.VMEM((pool.shape[0] + nb * 8, 512), F32),
            pltpu.VMEM((zpool.shape[0] + nb * 64, 128), F32),
            pltpu.VMEM((2, nb * 80, 1536), BF16),
            pltpu.VMEM((2, 3, 1536, 4 * outs), BF16),
        ],
        compiler_params=params(58),
    )(rows, field, pool, zpool, weight, mask_rows)


def merge(parts):
    sums = jnp.sum(parts[:, 0:1, :], axis=0)
    counts = jnp.sum(parts[:, 2:3, :], axis=0)
    mean = sums / jnp.maximum(counts, 1.0)
    gaps = parts[:, 0:1, :] / jnp.maximum(parts[:, 2:3, :], 1.0) - mean[None]
    squares = jnp.sum(parts[:, 1:2, :] + parts[:, 2:3, :] * gaps * gaps, axis=0)
    return sums, squares, counts


def stats_kernel(sections, lanes, stat_ref, out_ref, near, far, mid, send, recv, send2, recv2):
    s = lax.axis_index("corridor")
    g = lax.axis_index("group")
    barrier = pltpu.get_barrier_semaphore()

    def lane_peer(d):
        return (s, lax.rem(g + d, lanes))

    def section_peer(d):
        return (lax.rem(s + d, sections), g)

    @pl.loop(1, lanes)
    def _(d):
        pl.semaphore_signal(barrier, inc=1, device_id=lane_peer(d), device_id_type=MESH)

    @pl.loop(1, sections)
    def _(d):
        pl.semaphore_signal(barrier, inc=1, device_id=section_peer(d), device_id_type=MESH)

    pl.semaphore_wait(barrier, lanes + sections - 2)

    def exchange(src, dst, me, count, peer, send_sem, recv_sem):
        def copy(d, slot):
            return pltpu.make_async_remote_copy(
                src_ref=src, dst_ref=dst.at[slot], send_sem=send_sem.at[d],
                recv_sem=recv_sem.at[slot], device_id=peer(d), device_id_type=MESH,
            )

        @pl.loop(1, count)
        def _(d):
            copy(d, me).start()

        dst[me] = src[...]

        @pl.loop(1, count)
        def _(d):
            copy(d, lax.rem(me + count - d, count)).wait_recv()

        @pl.loop(1, count)
        def _(d):
            copy(d, me).wait_send()

    exchange(stat_ref, near, g, lanes, lane_peer, send, recv)
    sums, squares, counts = merge(near[...])
    mid[...] = jnp.zeros((8, 128), F32)
    mid[0:1, :] = sums
    mid[1:2, :] = squares
    mid[2:3, :] = counts
    exchange(mid, far, s, sections, section_peer, send2, recv2)
    sums, squares, counts = merge(far[...])
    out_ref[...] = jnp.zeros((8, 128), F32)
    out_ref[0:1, :] = sums / counts
    out_ref[1:2, :] = squares / counts


def global_stats(stat, collective):
    sections = lax.axis_size("corridor")
    lanes = lax.axis_size("group")
    return pl.pallas_call(
        functools.partial(stats_kernel, sections, lanes),
        out_shape=jax.ShapeDtypeStruct((8, 128), F32),
        in_specs=[VMEM],
        out_specs=VMEM,
        scratch_shapes=[
            pltpu.VMEM((lanes, 8, 128), F32),
            pltpu.VMEM((sections, 8, 128), F32),
            pltpu.VMEM((8, 128), F32),
            pltpu.SemaphoreType.DMA((lanes,)),
            pltpu.SemaphoreType.DMA((lanes,)),
            pltpu.SemaphoreType.DMA((sections,)),
            pltpu.SemaphoreType.DMA((sections,)),
        ],
        compiler_params=params(16, collective_id=collective, has_side_effects=True),
    )(stat)


def scaled(value, stat_ref, gain_ref, offset_ref):
    mean = stat_ref[0:1, :]
    deviation = value - mean
    root = jnp.sqrt(stat_ref[1:2, :] + 1e-05)
    return jnp.maximum(gain_ref[...] * deviation / root + offset_ref[...], 0.0)


def hidden_kernel(
    nb, v_ref, stat_ref, gain_ref, offset_ref, m_ref, field_ref, bundle_ref, z_ref, *tiles
):
    mask = spread(m_ref[...], 64)
    for t in range(4):
        span = slice(128 * t, 128 * t + 128)
        tiles[t][...] = scaled(v_ref[:, span], stat_ref, gain_ref, offset_ref) * mask[:, span]
    emit_field(nb, tiles, field_ref, bundle_ref, z_ref)


def make_hidden(first, stat, gain, offset, mask_rows):
    nb = first.shape[0] // 64
    return pl.pallas_call(
        functools.partial(hidden_kernel, nb),
        out_shape=field_shapes(nb),
        in_specs=[VMEM] * 5,
        out_specs=(VMEM, VMEM, VMEM),
        scratch_shapes=[pltpu.VMEM((nb * 64, 128), F32) for _ in range(4)],
        compiler_params=params(32),
    )(first, stat, gain, offset, mask_rows)


def final_kernel(v_ref, stat_ref, gain_ref, offset_ref, m_ref, out_ref, t_ref):
    for x in range(8):
        for z in range(8):
            t_ref[pl.ds(64 * x + z, 8, stride=8), :] = v_ref[x, :, 128 * z : 128 * z + 128]
    value = scaled(t_ref[...], stat_ref, gain_ref, offset_ref)
    out_ref[0] = (value.T * m_ref[0]).astype(BF16)


def make_output(second, stat, gain, offset, mask_f):
    nb = mask_f.shape[0]
    row = pl.BlockSpec((1, 128), lambda b: (0, 0))
    return pl.pallas_call(
        final_kernel,
        grid=(nb,),
        out_shape=jax.ShapeDtypeStruct((nb, 128, 512), BF16),
        in_specs=[
            pl.BlockSpec((8, 8, 1024), lambda b: (0, b, 0)),
            pl.BlockSpec((8, 128), lambda b: (0, 0)),
            row,
            row,
            pl.BlockSpec((1, 1, 512), lambda b: (b, 0, 0)),
        ],
        out_specs=pl.BlockSpec((1, 128, 512), lambda b: (b, 0, 0)),
        scratch_shapes=[pltpu.VMEM((512, 128), F32)],
        compiler_params=params(32),
    )(second.reshape(8, nb * 8, 1024), stat, gain, offset, mask_f.reshape(nb, 1, 512))


def share(bundle, zface):
    face = bundle.shape[0] // 4
    count = lax.axis_size("corridor")
    forward = [(i, i + 1) for i in range(count - 1)]
    backward = [(target, source) for source, target in forward]
    before = lax.ppermute(bundle[face : 2 * face], "corridor", forward)
    after = lax.ppermute(bundle[0:face], "corridor", backward)
    zpool = lax.all_gather(zface, "group", axis=0, tiled=True)
    pool = lax.all_gather(
        jnp.concatenate([bundle, before, after], axis=0), "group", axis=0, tiled=True
    )
    return pool, zpool


def shards(
    features, voxel_mask, neighbours, weight_first, gain_first, offset_first,
    weight_second, gain_second, offset_second,
):
    nb = features.shape[0]
    face = nb * 8
    lanes = lax.axis_size("group")
    corridor_at = lax.axis_index("corridor")
    mask_f = voxel_mask.astype(F32)
    mask_rows = voxel_mask.astype(BF16).reshape(nb, 8, 8, 8).transpose(1, 0, 2, 3)
    mask_rows = jnp.pad(mask_rows.reshape(nb * 64, 8), ((0, 0), (0, 120)))

    safe = jnp.maximum(neighbours, 0)
    owner = safe // nb
    slot = safe % nb
    same = owner // lanes == corridor_at
    lane = owner % lanes
    dx = jnp.array([[step[0] for step in DIRECTIONS]], jnp.int32)
    dy = jnp.array([[step[1] for step in DIRECTIONS]], jnp.int32)
    x_part = jnp.where(dx < 0, jnp.where(same, 1, 4), jnp.where(same, 0, 5)) * face + slot * 8
    y_part = jnp.where(dy < 0, 3, 2) * face + slot
    place = lane * (6 * face) + jnp.where(dx != 0, x_part, y_part)
    z_only = (dx == 0) & (dy == 0)
    place = jnp.where(z_only, lane * (8 * face) + slot * 8, place)
    nothing = jnp.where(z_only, lanes * 8 * face, lanes * 6 * face)
    rows = jnp.where(neighbours >= 0, place, nothing).astype(jnp.int32)

    w1 = weight_first.transpose(0, 2, 1).reshape(9, 3, 64, 64)
    w1 = jnp.concatenate(
        [jnp.pad(w1, ((0, 0), (0, 1), (0, 0), (0, 0))), jnp.pad(w1, ((0, 0), (1, 0), (0, 0), (0, 0)))],
        axis=3,
    ).reshape(9 * 4 * 64, 128)
    w2 = weight_second.transpose(0, 2, 1).reshape(27 * 64, 128)
    gain1 = jnp.tile(gain_first, 2)[None]
    offset1 = jnp.tile(offset_first, 2)[None]

    field, bundle, zface = prepare(features, mask_f)
    pool, zpool = share(bundle, zface)
    first, stat = conv(rows, field, pool, zpool, w1, mask_rows, lanes, 64)
    stat = global_stats(stat, 1)
    field, bundle, zface = make_hidden(first, stat, gain1, offset1, mask_rows)
    pool, zpool = share(bundle, zface)
    second, stat = conv(rows, field, pool, zpool, w2, mask_rows, lanes, 128)
    stat = global_stats(stat, 1)
    return make_output(second, stat, gain_second[None], offset_second[None], mask_f)


def solution(mesh):
    in_specs = (
        P(("corridor", "group"), None, None),
        P(("corridor", "group"), None),
        P(("corridor", "group"), None),
        P(),
        P(),
        P(),
        P(),
        P(),
        P(),
    )
    out_specs = P(("corridor", "group"), None, None)
    return jax.shard_map(shards, mesh=mesh, in_specs=in_specs, out_specs=out_specs, check_vma=False)
```

time: 1120 us -> 149 us (0.13); the launches traced: 1100 us -> 148 us
  local copies, waits for them, and re-layouts: 540 us -> 9.08 us
  matrix products: 189 us -> 0 us
  blocking collectives: 161 us -> 18.4 us
  other arithmetic: 146 us -> 4.32 us
  Pallas kernels: 0 us -> 53.7 us
    reshape x65 -> x3, local copies, waits for them, and re-layouts: 206 us -> 0.53 us  [the longest x1 0.26 us: shards(): voxel_mask.astype(BF16).reshape(nb, 8, 8, 8).transpose(1, 0, 2, 3)]
    dot_general x54 -> x0, matrix products: 189 us -> none  [conv_layer(): jnp.einsum('oc,bcxyz->boxyz', weight[tap], padded[:, :, oa:oa + 8, oe:oe...]
    psum x4 -> x0, blocking collectives: 161 us -> none  [the longest x2 82.3 us: normalize(): var = lax.psum(local_square, ('corridor', 'group')) / count]
    slice x48 -> x2, local copies, waits for them, and re-layouts: 118 us -> 0.03 us  [share(): before = lax.ppermute(bundle[face:2 * face], 'corridor', forward)]
    unnamed x250 -> x38, local copies, waits for them, and re-layouts: 94.5 us -> 7.58 us
    scatter x52 -> x0, other arithmetic: 66.2 us -> none  [conv_layer(): padded = padded.at[:, :, rx[2]:rx[2] + rx[1] - rx[0], ry[2]:ry[2] + ry[1]...]
    another operation x6 -> x4, local copies, waits for them, and re-layouts: 55 us -> 0.17 us  [the longest x2 0.09 us: shards(): offset1 = jnp.tile(offset_first, 2)[None]]
    pallas_call x0 -> x7, Pallas kernels: none -> 53.7 us  [the longest x2 27.1 us: conv(): pl.pallas_call(functools.partial(conv_kernel, nb, lanes, outs), out_shape...]
  transfers between devices with their start and end apart: 6 -> 6, of which waited for: 2 -> 6; matrix products, arithmetic and copies ran while one was open for 8% -> 2% of each run, Pallas kernels for 0% -> 0%
where the time goes in v1:
time: 149 us; the launch traced here: 148 us
  Pallas kernels  53.7 us (36%)
  waiting for transfers between devices  38.4 us (26%)
  blocking collectives  18.4 us (12%)
  between operations  13.7 us (9%)
  starting transfers between devices  10.9 us (7%)
  local copies, waits for them, and re-layouts  9.08 us (6%)
  other arithmetic  4.32 us (3%)
    all_gather x2, waiting for transfers between devices, share(): lax.all_gather(jnp.concatenate([bundle, before, after], axis=0), 'group',...  27.9 us
    pallas_call x2, Pallas kernels, conv(): pl.pallas_call(functools.partial(conv_kernel, nb, lanes, outs), out_shape...  27.1 us
    pallas_call x2, Pallas kernels, global_stats(): pl.pallas_call(functools.partial(stats_kernel, sections, lanes), out_shap...  19.7 us
    all_gather x2, blocking collectives, share(): zpool = lax.all_gather(zface, 'group', axis=0, tiled=True)  18.4 us
    ppermute x2, waiting for transfers between devices, share(): after = lax.ppermute(bundle[0:face], 'corridor', backward)  8.78 us
    ppermute x2, starting transfers between devices, share(): before = lax.ppermute(bundle[face:2 * face], 'corridor', forward)  8.1 us
    unnamed x38, local copies, waits for them, and re-layouts  7.58 us
    pallas_call x1, Pallas kernels, make_output(): pl.pallas_call(final_kernel, grid=(nb,), out_shape=jax.ShapeDtypeStruct((...  5.29 us
  transfers between devices with their start and end apart: 6, of which 6 were waited for; matrix products, arithmetic and copies ran while one was open for 2% of the time, Pallas kernels for 0%

profile of v1, /device:TPU:0, one launch (start us, length us, event | category | flops | bytes accessed | tf_op | source)
XLA Modules:
  0.0 148.4 jit_solution(2670163428910234087)
XLA Ops:
  7.4 1.1 copy-done.5
  8.5 1.0 shard_map.109
  9.5 0.9 copy-done.3
  10.4 4.8 %collective-permute-start = (bf16[96,512]{1,0:T(8,128)(2,1)S(1)}, bf16[96,512]{1,0:T(8,128)(2,1)S(1)}, u32[]{:S(2)}, u32[]{:S(2)}) collective-permute-start(bf16[96,512]{1,0:T(8,128)(2,1)S(1)} %get-tuple-element.27), channel_id=1, source_target_pairs={{0,4},{4,8},{8,12},{12,16},{16,20},{20,24},{24,28},{1,5},{5,9},{9,... | collective-permute-start | bytes 294920 | tf_op jit(solution)/shard_map/ppermute | solution.py:391
  15.3 1.4 collective-permute-start.1
  17.5 4.5 %collective-permute-done.1 = bf16[96,512]{1,0:T(8,128)(2,1)S(1)} collective-permute-done((bf16[96,512]{1,0:T(8,128)(2,1)S(1)}, bf16[96,512]{1,0:T(8,128)(2,1)S(1)}, u32[]{:S(2)}, u32[]{:S(2)}) %collective-permute-start.1) | collective-permute-done | bytes 98336 | tf_op jit(solution)/shard_map/ppermute | solution.py:392
  21.9 0.9 pad_maximum_fusion
  24.4 1.2 fusion.2
  26.3 9.1 %all_gather.13.zpool_ref = bf16[3072,128]{1,0:T(8,128)(2,1)} all-gather(bf16[768,128]{1,0:T(8,128)(2,1)S(1)} %get-tuple-element.17), channel_id=1, replica_groups=mesh['corridor'=8,'group'=4] {'group'}, dimensions={0}, use_global_device_ids=true | all-gather | bytes 983040 | tf_op jit(solution)/shard_map/all_gather | solution.py:393
  35.3 12.9 %all-gather.3.cloned.1.call-done.pool_ref = bf16[2304,512]{1,0:T(8,128)(2,1)} async-done(((bf16[576,512]{1,0:T(8,128)(2,1)}), bf16[2304,512]{1,0:T(8,128)(2,1)}) %all-gather.3.cloned.1.call-update) | async-done | bytes 2359312 | tf_op jit(solution)/shard_map/all_gather | solution.py:394
  48.2 11.2 %shard_map.110 = (f32[768,512]{1,0:T(8,128)}, f32[8,128]{1,0:T(8,128)}) custom-call(s32[12,26]{1,0:T(8,128)} %select_select_fusion.rows_ref, bf16[768,512]{1,0:T(8,128)(2,1)} %copy-done.3, bf16[2304,512]{1,0:T(8,128)(2,1)} %all-gather.3.cloned.1.call-done.pool_ref, bf16[3072,128]{1,0:T(8,128)(2,1)} %all_gather.13.zpool_ref, bf16[2304,128]{1,0:T(8,128)(2,1)} %bitcast.15, ...), custom_call_target="tpu_custom_call" | custom-call | tf_op jit(solution)/shard_map/pallas_call | solution.py:225
  60.1 10.0 %shard_map.111.stat_ref = f32[8,128]{1,0:T(8,128)S(1)} custom-call(f32[8,128]{1,0:T(8,128)S(1)} %copy-done.7), custom_call_target="tpu_custom_call" | custom-call | tf_op jit(solution)/shard_map/pallas_call | solution.py:311
  70.1 1.4 copy-done.2
  72.1 0.9 copy-done.4
  73.0 3.3 %collective-permute-start.2 = (bf16[96,512]{1,0:T(8,128)(2,1)S(1)}, bf16[96,512]{1,0:T(8,128)(2,1)S(1)}, u32[]{:S(2)}, u32[]{:S(2)}) collective-permute-start(bf16[96,512]{1,0:T(8,128)(2,1)S(1)} %get-tuple-element.25), channel_id=1, source_target_pairs={{0,4},{4,8},{8,12},{12,16},{16,20},{20,24},{24,28},{1,5},{5,9},{9,... | collective-permute-start | bytes 294920 | tf_op jit(solution)/shard_map/ppermute | solution.py:391
  76.3 1.3 collective-permute-start.3
  77.6 0.9 collective-permute-done.2
  78.5 4.3 %collective-permute-done.3 = bf16[96,512]{1,0:T(8,128)(2,1)S(1)} collective-permute-done((bf16[96,512]{1,0:T(8,128)(2,1)S(1)}, bf16[96,512]{1,0:T(8,128)(2,1)S(1)}, u32[]{:S(2)}, u32[]{:S(2)}) %collective-permute-start.3) | collective-permute-done | bytes 98336 | tf_op jit(solution)/shard_map/ppermute | solution.py:392
  83.7 9.3 %all_gather.15.zpool_ref = bf16[3072,128]{1,0:T(8,128)(2,1)} all-gather(bf16[768,128]{1,0:T(8,128)(2,1)S(1)} %get-tuple-element.22), channel_id=1, replica_groups=mesh['corridor'=8,'group'=4] {'group'}, dimensions={0}, use_global_device_ids=true | all-gather | bytes 983040 | tf_op jit(solution)/shard_map/all_gather | solution.py:393
  93.0 15.0 %all-gather.5.cloned.1.call-done.pool_ref = bf16[2304,512]{1,0:T(8,128)(2,1)} async-done(((bf16[576,512]{1,0:T(8,128)(2,1)}), bf16[2304,512]{1,0:T(8,128)(2,1)}) %all-gather.5.cloned.1.call-update) | async-done | bytes 2359312 | tf_op jit(solution)/shard_map/all_gather | solution.py:394
  108.0 15.9 %shard_map.113 = (f32[768,1024]{1,0:T(8,128)}, f32[8,128]{1,0:T(8,128)}) custom-call(s32[12,26]{1,0:T(8,128)} %select_select_fusion.rows_ref, bf16[768,512]{1,0:T(8,128)(2,1)} %copy-done.4, bf16[2304,512]{1,0:T(8,128)(2,1)} %all-gather.5.cloned.1.call-done.pool_ref, bf16[3072,128]{1,0:T(8,128)(2,1)} %all_gather.15.zpool_ref, bf16[1728,128]{1,0:T(8,128)(2,1)} %bitcast.18, ...), custom_call_target="tpu_custom_call" | custom-call | tf_op jit(solution)/shard_map/pallas_call | solution.py:225
  124.6 9.7 %shard_map.114.stat_ref = f32[8,128]{1,0:T(8,128)S(1)} custom-call(f32[8,128]{1,0:T(8,128)S(1)} %copy-done.6), custom_call_target="tpu_custom_call" | custom-call | tf_op jit(solution)/shard_map/pallas_call | solution.py:311
  134.4 1.9 %copy-done.1 = f32[768,1024]{1,0:T(8,128)S(1)} copy-done((f32[768,1024]{1,0:T(8,128)S(1)}, f32[768,1024]{1,0:T(8,128)}, u32[]{:S(2)}) %copy-start.1) | copy-done | bytes 3145752
  136.2 5.3 %shard_map.115 = bf16[12,128,512]{2,1,0:T(8,128)(2,1)} custom-call(f32[8,96,1024]{2,1,0:T(8,128)S(1)} %bitcast.12, f32[8,128]{1,0:T(8,128)S(1)} %shard_map.114.stat_ref, f32[1,128]{1,0:T(1,128)S(1)} %bitcast.13, f32[1,128]{1,0:T(1,128)S(1)} %bitcast.14, f32[12,1,512]{2,1,0:T(1,128)S(1)} %reshape.29.m_ref), custom_call_target="tpu_custom_call" | custom-call | tf_op jit(solution)/shard_map/pallas_call | solution.py:369
  (53 shorter events, 6.7 us)
Async XLA Ops:
  6.5 41.7 %all-gather.3.cloned.1.call-start = ((), (), s32[]{:S(2)}) async-start(), calls=%async_computation | async-start | bytes 2949120 | tf_op jit(solution)/shard_map/all_gather | solution.py:394
  7.4 1.1 copy-start.5
  9.5 0.9 copy-start.3
  10.4 12.5 %copy-start.17 = (f32[64]{0:T(128)S(1)}, f32[64]{0:T(128)}, u32[]{:S(2)}) copy-start(f32[64]{0:T(128)} %param.15) | copy-start | bytes 772
  10.4 12.6 %copy-start.18 = (f32[64]{0:T(128)S(1)}, f32[64]{0:T(128)}, u32[]{:S(2)}) copy-start(f32[64]{0:T(128)} %param.16) | copy-start | bytes 772
  10.4 7.0 %collective-permute-start = (bf16[96,512]{1,0:T(8,128)(2,1)S(1)}, bf16[96,512]{1,0:T(8,128)(2,1)S(1)}, u32[]{:S(2)}, u32[]{:S(2)}) collective-permute-start(bf16[96,512]{1,0:T(8,128)(2,1)S(1)} %get-tuple-element.27), channel_id=1, source_target_pairs={{0,4},{4,8},{8,12},{12,16},{16,20},{20,24},{24,28},{1,5},{5,9},{9,... | collective-permute-start | bytes 294920 | tf_op jit(solution)/shard_map/ppermute | solution.py:391
  15.3 8.2 %copy-start.10 = (bf16[27,64,64]{2,1,0:T(8,128)(2,1)S(1)}, bf16[27,64,64]{2,1,0:T(8,128)(2,1)}, u32[]{:S(2)}) copy-start(bf16[27,64,64]{2,1,0:T(8,128)(2,1)} %param.14) | copy-start | bytes 663556
  15.3 6.6 %collective-permute-start.1 = (bf16[96,512]{1,0:T(8,128)(2,1)S(1)}, bf16[96,512]{1,0:T(8,128)(2,1)S(1)}, u32[]{:S(2)}, u32[]{:S(2)}) collective-permute-start(bf16[96,512]{1,0:T(8,128)(2,1)S(1)} %get-tuple-element.28), channel_id=1, source_target_pairs={{4,0},{8,4},{12,8},{16,12},{20,16},{24,20},{28,24},{5,1},{9,5},{13... | collective-permute-start | bytes 294920 | tf_op jit(solution)/shard_map/ppermute | solution.py:392
  22.8 85.2 %all-gather.5.cloned.1.call-start = ((), (), s32[]{:S(2)}) async-start(), calls=%async_computation.1 | async-start | bytes 2949120 | tf_op jit(solution)/shard_map/all_gather | solution.py:394
  23.4 2.2 %copy-start.11 = (s32[12,26]{1,0:T(8,128)S(1)}, s32[12,26]{1,0:T(8,128)}, u32[]{:S(2)}) copy-start(s32[12,26]{1,0:T(8,128)} %param.13) | copy-start | bytes 3748
  23.4 2.2 %copy-start.12 = (s32[26]{0:T(128)S(1)}, s32[26]{0:T(128)}, u32[]{:S(2)}) copy-start(s32[26]{0:T(128)} %constant.97) | copy-start | bytes 316
  23.4 2.2 %copy-start.13 = (s32[26]{0:T(128)S(1)}, s32[26]{0:T(128)}, u32[]{:S(2)}) copy-start(s32[26]{0:T(128)} %constant.95) | copy-start | bytes 316
  23.4 2.2 %copy-start.14 = (pred[26]{0:T(512)(128)(4,1)S(1)}, pred[26]{0:T(512)(128)(4,1)}, u32[]{:S(2)}) copy-start(pred[26]{0:T(512)(128)(4,1)} %constant.91) | copy-start | bytes 82
  23.4 2.2 %copy-start.15 = (pred[26]{0:T(512)(128)(4,1)S(1)}, pred[26]{0:T(512)(128)(4,1)}, u32[]{:S(2)}) copy-start(pred[26]{0:T(512)(128)(4,1)} %constant.89) | copy-start | bytes 82
  23.4 2.2 %copy-start.16 = (pred[26]{0:T(512)(128)(4,1)S(1)}, pred[26]{0:T(512)(128)(4,1)}, u32[]{:S(2)}) copy-start(pred[26]{0:T(512)(128)(4,1)} %constant.87) | copy-start | bytes 82
  48.2 21.9 %copy-start = (bf16[768,128]{1,0:T(8,128)(2,1)S(1)}, bf16[768,128]{1,0:T(8,128)(2,1)}, u32[]{:S(2)}) copy-start(bf16[768,128]{1,0:T(8,128)(2,1)} %pad.14.m_ref) | copy-start | bytes 589828
  70.1 1.4 copy-start.2
  72.1 0.9 copy-start.4
  73.0 5.5 %collective-permute-start.2 = (bf16[96,512]{1,0:T(8,128)(2,1)S(1)}, bf16[96,512]{1,0:T(8,128)(2,1)S(1)}, u32[]{:S(2)}, u32[]{:S(2)}) collective-permute-start(bf16[96,512]{1,0:T(8,128)(2,1)S(1)} %get-tuple-element.25), channel_id=1, source_target_pairs={{0,4},{4,8},{8,12},{12,16},{16,20},{20,24},{24,28},{1,5},{5,9},{9,... | collective-permute-start | bytes 294920 | tf_op jit(solution)/shard_map/ppermute | solution.py:391
  76.3 6.5 %collective-permute-start.3 = (bf16[96,512]{1,0:T(8,128)(2,1)S(1)}, bf16[96,512]{1,0:T(8,128)(2,1)S(1)}, u32[]{:S(2)}, u32[]{:S(2)}) collective-permute-start(bf16[96,512]{1,0:T(8,128)(2,1)S(1)} %get-tuple-element.26), channel_id=1, source_target_pairs={{4,0},{8,4},{12,8},{16,12},{20,16},{24,20},{28,24},{5,1},{9,5},{13... | collective-permute-start | bytes 294920 | tf_op jit(solution)/shard_map/ppermute | solution.py:392
  108.0 26.3 %copy-start.8 = (f32[128]{0:T(128)S(1)}, f32[128]{0:T(128)}, u32[]{:S(2)}) copy-start(f32[128]{0:T(128)} %param.18) | copy-start | bytes 1540
  108.0 26.3 %copy-start.9 = (f32[128]{0:T(128)S(1)}, f32[128]{0:T(128)}, u32[]{:S(2)}) copy-start(f32[128]{0:T(128)} %param.19) | copy-start | bytes 1540
  123.9 0.7 copy-start.6
  134.3 1.9 %copy-start.1 = (f32[768,1024]{1,0:T(8,128)S(1)}, f32[768,1024]{1,0:T(8,128)}, u32[]{:S(2)}) copy-start(f32[768,1024]{1,0:T(8,128)} %get-tuple-element.23) | copy-start | bytes 9437188
  (1 other events, 0.7 us)
Sparse Core Ops, SparseCore 0:
  22.9 25.2 all-gather.2
  83.8 24.1 all-gather.4

commit v2 on v1

--- a/solution.py
+++ b/solution.py
@@ -383,18 +383,126 @@
     )(second.reshape(8, nb * 8, 1024), stat, gain, offset, mask_f.reshape(nb, 1, 512))
 
 
+def halo_kernel(sections, lanes, face, bundle_ref, z_ref, pool_ref, zpool_ref, send, recv):
+    s = lax.axis_index("corridor")
+    g = lax.axis_index("group")
+    half = lanes // 2
+    other = g + 1 - 2 * lax.rem(g, 2)
+    has = {2: s > 0, 3: s < sections - 1}
+    far_lanes = [lax.rem(g + 2 * j, lanes) for j in range(1, half)]
+    mirror = [lax.rem(other + 2 * j, lanes) for j in range(1, half)]
+
+    def place(k, lane):
+        if k == 1:
+            return zpool_ref.at[pl.ds(pl.multiple_of(lane * (8 * face), 16), 8 * face), :]
+        start, size = {0: (0, 4 * face), 2: (4 * face, face), 3: (5 * face, face)}[k]
+        return pool_ref.at[pl.ds(pl.multiple_of(lane * (6 * face) + start, 16), size), :]
+
+    def copy(k, lane, src, peer, slot):
+        return pltpu.make_async_remote_copy(
+            src_ref=src, dst_ref=place(k, lane), send_sem=send.at[slot],
+            recv_sem=recv.at[k * lanes + lane], device_id=peer, device_id_type=MESH,
+        )
+
+    def across(k, j):
+        src = {0: bundle_ref, 1: z_ref}.get(k)
+        return copy(k, g, place(k, g) if src is None else src, (s, far_lanes[j]), j * 4 + k)
+
+    def beside(k, j):
+        lane = g if j == 0 else far_lanes[j - 1]
+        src = {0: bundle_ref, 1: z_ref}.get(k) if j == 0 else None
+        return copy(
+            k, lane, place(k, lane) if src is None else src, (s, other), (half + j) * 4 + k
+        )
+
+    def arrive(k, lane):
+        copy(k, lane, place(k, lane), (s, other), 0).wait_recv()
+
+    def along(k):
+        rows = pl.ds(face, face) if k == 2 else pl.ds(0, face)
+        target = s + 1 if k == 2 else s - 1
+        return copy(k, g, bundle_ref.at[rows, :], (target, g), 8 * half + k)
+
+    def guarded(k, action):
+        if k in has:
+            pl.when(has[k])(action)
+        else:
+            action()
+
+    barrier = pltpu.get_barrier_semaphore()
+
+    def greet(peer):
+        pl.semaphore_signal(barrier, inc=1, device_id=peer, device_id_type=MESH)
+
+    greet((s, other))
+    for lane in far_lanes:
+        greet((s, lane))
+    guarded(2, lambda: greet((s - 1, g)))
+    guarded(3, lambda: greet((s + 1, g)))
+    ends = jnp.where(s > 0, 1, 0) + jnp.where(s < sections - 1, 1, 0)
+    pl.semaphore_wait(barrier, half + ends)
+
+    guarded(3, lambda: along(2).start())
+    guarded(2, lambda: along(3).start())
+    for k in (0, 1):
+        for j in range(half - 1):
+            across(k, j).start()
+    for k in (0, 1):
+        beside(k, 0).start()
+    pool_ref[pl.ds(pl.multiple_of(g * (6 * face), 16), 4 * face), :] = bundle_ref[...]
+    zpool_ref[pl.ds(pl.multiple_of(g * (8 * face), 16), 8 * face), :] = z_ref[...]
+
+    def pass_on(k):
+        def action():
+            arrive(k, g)
+            for j in range(half - 1):
+                across(k, j).start()
+            beside(k, 0).start()
+
+        return action
+
+    def relay(k, j):
+        def action():
+            arrive(k, far_lanes[j])
+            beside(k, j + 1).start()
+
+        return action
+
+    for k in (2, 3):
+        guarded(k, pass_on(k))
+    for k in range(4):
+        for j in range(half - 1):
+            guarded(k, relay(k, j))
+    for k in range(4):
+        for lane in [other] + mirror:
+            guarded(k, lambda k=k, lane=lane: arrive(k, lane))
+    guarded(3, lambda: along(2).wait_send())
+    guarded(2, lambda: along(3).wait_send())
+    for k in range(4):
+        for j in range(half - 1):
+            guarded(k, lambda k=k, j=j: across(k, j).wait_send())
+        for j in range(half):
+            guarded(k, lambda k=k, j=j: beside(k, j).wait_send())
+
+
 def share(bundle, zface):
     face = bundle.shape[0] // 4
-    count = lax.axis_size("corridor")
-    forward = [(i, i + 1) for i in range(count - 1)]
-    backward = [(target, source) for source, target in forward]
-    before = lax.ppermute(bundle[face : 2 * face], "corridor", forward)
-    after = lax.ppermute(bundle[0:face], "corridor", backward)
-    zpool = lax.all_gather(zface, "group", axis=0, tiled=True)
-    pool = lax.all_gather(
-        jnp.concatenate([bundle, before, after], axis=0), "group", axis=0, tiled=True
-    )
-    return pool, zpool
+    sections = lax.axis_size("corridor")
+    lanes = lax.axis_size("group")
+    return pl.pallas_call(
+        functools.partial(halo_kernel, sections, lanes, face),
+        out_shape=(
+            jax.ShapeDtypeStruct((lanes * 6 * face, 512), BF16),
+            jax.ShapeDtypeStruct((lanes * 8 * face, 128), BF16),
+        ),
+        in_specs=[VMEM, VMEM],
+        out_specs=(VMEM, VMEM),
+        scratch_shapes=[
+            pltpu.SemaphoreType.DMA((4 * lanes + 4,)),
+            pltpu.SemaphoreType.DMA((4 * lanes,)),
+        ],
+        compiler_params=params(32, collective_id=2, has_side_effects=True),
+    )(bundle, zface)
 
 
 def shards(

time: 149 us -> 114 us (0.77)
  Pallas kernels: 53.7 us -> 96.1 us
  waiting for transfers between devices: 38.4 us -> 0 us
  blocking collectives: 18.4 us -> 0 us
  between operations: 13.7 us -> 0.16 us
  starting transfers between devices: 10.9 us -> 0 us
  local copies, waits for them, and re-layouts: 9.08 us -> 13.9 us
    pallas_call x0 -> x2, Pallas kernels: none -> 39.7 us  [share(): pl.pallas_call(functools.partial(halo_kernel, sections, lanes, face), out...]
    all_gather x2 -> x0, waiting for transfers between devices: 27.9 us -> none  [share(): lax.all_gather(jnp.concatenate([bundle, before, after], axis=0), 'group',...]
    all_gather x2 -> x0, blocking collectives: 18.4 us -> none  [share(): zpool = lax.all_gather(zface, 'group', axis=0, tiled=True)]
    ppermute x4 -> x0, starting transfers between devices: 10.8 us -> none  [the longest x2 8.1 us: share(): before = lax.ppermute(bundle[face:2 * face], 'corridor', forward)]
    ppermute x4 -> x0, waiting for transfers between devices: 10.4 us -> none  [the longest x2 8.78 us: share(): after = lax.ppermute(bundle[0:face], 'corridor', backward)]
    unnamed x38 -> x30, local copies, waits for them, and re-layouts: 7.58 us -> 11.1 us
    pallas_call x2, Pallas kernels: 19.7 us -> 22.4 us  [global_stats(): pl.pallas_call(functools.partial(stats_kernel, sections, lanes), out_shap...]
    concatenate x2 -> x0, other arithmetic: 1.7 us -> none  [share(): jnp.concatenate([bundle, before, after], axis=0)]
  transfers between devices with their start and end apart: 6 -> 0, of which waited for: 6 -> 0; matrix products, arithmetic and copies ran while one was open for 2% -> 0% of each run, Pallas kernels for 0% -> 0%
where the time goes in v2:
time: 114 us; the launch traced here: 113 us
  Pallas kernels  96.1 us (84%)
  local copies, waits for them, and re-layouts  13.9 us (12%)
  other arithmetic  3.36 us (3%)
    pallas_call x2, Pallas kernels, share(): pl.pallas_call(functools.partial(halo_kernel, sections, lanes, face), out...  39.7 us
    pallas_call x2, Pallas kernels, conv(): pl.pallas_call(functools.partial(conv_kernel, nb, lanes, outs), out_shape...  27.1 us
    pallas_call x2, Pallas kernels, global_stats(): pl.pallas_call(functools.partial(stats_kernel, sections, lanes), out_shap...  22.4 us
    unnamed x30, local copies, waits for them, and re-layouts  11.1 us
    pallas_call x1, Pallas kernels, make_output(): pl.pallas_call(final_kernel, grid=(nb,), out_shape=jax.ShapeDtypeStruct((...  5.29 us

profile of v2, /device:TPU:0, one launch (start us, length us, event | category | flops | bytes accessed | tf_op | source)
XLA Modules:
  0.0 113.5 jit_solution(16632218491794981697)
XLA Ops:
  0.0 0.7 tile.4
  0.8 0.7 tile.5
  1.5 1.4 %select_select_fusion.rows_ref = s32[12,26]{1,0:T(8,128)} fusion(s32[12,26]{1,0:T(8,128)} %param.13, s32[26]{0:T(128)} %constant.97, s32[26]{0:T(128)} %constant.95, s32[]{:T(128)S(6)} %axis_index.15, pred[26]{0:T(512)(128)(4,1)} %constant.91, pred[26]{0:T(512)(128)(4,1)} %constant.89, pred[26]{0:T(512)(128)(4,1)} %constant.87), kind=kLoop, calls=%fused_computation.13 | loop fusion | flops 14976 | bytes 2786 | tf_op jit(solution)/shard_map/jit(_where)/select_n | solution.py:533
  2.9 0.8 fusion.7
  4.1 0.7 pad.14.m_ref
  5.0 1.2 %fusion.2 = bf16[9,4,64,128]{3,2,1,0:T(8,128)(2,1)} fusion(bf16[9,3,64,64]{3,2,1,0:T(8,128)(2,1)S(1)} %copy.15), kind=kLoop, calls=%fused_computation.4 | loop fusion | flops 2359296 | bytes 811008 | tf_op jit(solution)/shard_map/concatenate | solution.py:536
  6.2 1.0 shard_map.109
  7.2 0.9 copy-done.6
  8.1 20.9 %shard_map.110 = (bf16[2304,512]{1,0:T(8,128)(2,1)S(1)}, bf16[3072,128]{1,0:T(8,128)(2,1)S(1)}) custom-call(bf16[384,512]{1,0:T(8,128)(2,1)S(1)} %get-tuple-element.20.bundle_ref, bf16[768,128]{1,0:T(8,128)(2,1)S(1)} %get-tuple-element.21.z_ref), custom_call_target="tpu_custom_call" | custom-call | tf_op jit(solution)/shard_map/pallas_call | solution.py:492
  29.0 1.4 %copy-done.3 = bf16[2304,512]{1,0:T(8,128)(2,1)} copy-done((bf16[2304,512]{1,0:T(8,128)(2,1)}, bf16[2304,512]{1,0:T(8,128)(2,1)S(1)}, u32[]{:S(2)}) %copy-start.3) | copy-done | bytes 2359320
  30.4 0.9 copy-done.8
  31.3 11.2 %shard_map.111 = (f32[768,512]{1,0:T(8,128)}, f32[8,128]{1,0:T(8,128)}) custom-call(s32[12,26]{1,0:T(8,128)} %select_select_fusion.rows_ref, bf16[768,512]{1,0:T(8,128)(2,1)} %copy-done.6, bf16[2304,512]{1,0:T(8,128)(2,1)} %copy-done.3, bf16[3072,128]{1,0:T(8,128)(2,1)} %copy-done.8, bf16[2304,128]{1,0:T(8,128)(2,1)} %bitcast.15, bf16[768,128]{1,0:T(8,128)(2,1)} %pad.14.m_ref), custom_call_target="tpu_custom_call" | custom-call | tf_op jit(solution)/shard_map/pallas_call | solution.py:225
  42.5 0.7 copy-done.11
  43.1 11.4 %shard_map.112.stat_ref = f32[8,128]{1,0:T(8,128)S(1)} custom-call(f32[8,128]{1,0:T(8,128)S(1)} %copy-done.11), custom_call_target="tpu_custom_call" | custom-call | tf_op jit(solution)/shard_map/pallas_call | solution.py:311
  54.5 1.4 %copy-done.4 = f32[768,512]{1,0:T(8,128)S(1)} copy-done((f32[768,512]{1,0:T(8,128)S(1)}, f32[768,512]{1,0:T(8,128)}, u32[]{:S(2)}) %copy-start.4) | copy-done | bytes 1572888
  56.5 0.9 copy-done.5
  57.4 18.9 %shard_map.114 = (bf16[2304,512]{1,0:T(8,128)(2,1)S(1)}, bf16[3072,128]{1,0:T(8,128)(2,1)S(1)}) custom-call(bf16[384,512]{1,0:T(8,128)(2,1)S(1)} %get-tuple-element.27.bundle_ref, bf16[768,128]{1,0:T(8,128)(2,1)S(1)} %get-tuple-element.28.z_ref), custom_call_target="tpu_custom_call" | custom-call | tf_op jit(solution)/shard_map/pallas_call | solution.py:492
  76.3 1.4 %copy-done.2 = bf16[2304,512]{1,0:T(8,128)(2,1)} copy-done((bf16[2304,512]{1,0:T(8,128)(2,1)}, bf16[2304,512]{1,0:T(8,128)(2,1)S(1)}, u32[]{:S(2)}) %copy-start.2) | copy-done | bytes 2359320
  77.7 0.9 copy-done.7
  78.6 15.9 %shard_map.115 = (f32[768,1024]{1,0:T(8,128)}, f32[8,128]{1,0:T(8,128)}) custom-call(s32[12,26]{1,0:T(8,128)} %select_select_fusion.rows_ref, bf16[768,512]{1,0:T(8,128)(2,1)} %copy-done.5, bf16[2304,512]{1,0:T(8,128)(2,1)} %copy-done.2, bf16[3072,128]{1,0:T(8,128)(2,1)} %copy-done.7, bf16[1728,128]{1,0:T(8,128)(2,1)} %bitcast.18, bf16[768,128]{1,0:T(8,128)(2,1)} %pad.14.m_ref), custom_call_target="tpu_custom_call" | custom-call | tf_op jit(solution)/shard_map/pallas_call | solution.py:225
  94.6 0.7 copy-done.10
  95.2 11.0 %shard_map.116.stat_ref = f32[8,128]{1,0:T(8,128)S(1)} custom-call(f32[8,128]{1,0:T(8,128)S(1)} %copy-done.10), custom_call_target="tpu_custom_call" | custom-call | tf_op jit(solution)/shard_map/pallas_call | solution.py:311
  106.3 1.9 %copy-done.1 = f32[768,1024]{1,0:T(8,128)S(1)} copy-done((f32[768,1024]{1,0:T(8,128)S(1)}, f32[768,1024]{1,0:T(8,128)}, u32[]{:S(2)}) %copy-start.1) | copy-done | bytes 3145752
  108.2 5.3 %shard_map.117 = bf16[12,128,512]{2,1,0:T(8,128)(2,1)} custom-call(f32[8,96,1024]{2,1,0:T(8,128)S(1)} %bitcast.12, f32[8,128]{1,0:T(8,128)S(1)} %shard_map.116.stat_ref, f32[1,128]{1,0:T(1,128)S(1)} %bitcast.13, f32[1,128]{1,0:T(1,128)S(1)} %bitcast.14, f32[12,1,512]{2,1,0:T(1,128)S(1)} %reshape.29.m_ref), custom_call_target="tpu_custom_call" | custom-call | tf_op jit(solution)/shard_map/pallas_call | solution.py:369
  (27 shorter events, 1.4 us)
Async XLA Ops:
  0.0 4.8 %copy-start.14 = (bf16[27,64,64]{2,1,0:T(8,128)(2,1)S(1)}, bf16[27,64,64]{2,1,0:T(8,128)(2,1)}, u32[]{:S(2)}) copy-start(bf16[27,64,64]{2,1,0:T(8,128)(2,1)} %param.14) | copy-start | bytes 663556
  4.1 2.1 %copy-start.9 = (bf16[12,64,512]{2,1,0:T(8,128)(2,1)S(1)}, bf16[12,64,512]{2,1,0:T(8,128)(2,1)}, u32[]{:S(2)}) copy-start(bf16[12,64,512]{2,1,0:T(8,128)(2,1)} %x_ref.1) | copy-start | bytes 2359300
  7.2 0.9 copy-start.6
  29.0 1.4 %copy-start.3 = (bf16[2304,512]{1,0:T(8,128)(2,1)}, bf16[2304,512]{1,0:T(8,128)(2,1)S(1)}, u32[]{:S(2)}) copy-start(bf16[2304,512]{1,0:T(8,128)(2,1)S(1)} %get-tuple-element.22.pool_ref) | copy-start | bytes 7077892
  30.4 0.9 copy-start.8
  31.3 23.2 %copy-start = (bf16[768,128]{1,0:T(8,128)(2,1)S(1)}, bf16[768,128]{1,0:T(8,128)(2,1)}, u32[]{:S(2)}) copy-start(bf16[768,128]{1,0:T(8,128)(2,1)} %pad.14.m_ref) | copy-start | bytes 589828
  42.5 0.7 copy-start.11
  54.5 1.4 %copy-start.4 = (f32[768,512]{1,0:T(8,128)S(1)}, f32[768,512]{1,0:T(8,128)}, u32[]{:S(2)}) copy-start(f32[768,512]{1,0:T(8,128)} %get-tuple-element.24.v_ref) | copy-start | bytes 4718596
  56.5 0.9 copy-start.5
  76.3 1.4 %copy-start.2 = (bf16[2304,512]{1,0:T(8,128)(2,1)}, bf16[2304,512]{1,0:T(8,128)(2,1)S(1)}, u32[]{:S(2)}) copy-start(bf16[2304,512]{1,0:T(8,128)(2,1)S(1)} %get-tuple-element.29.pool_ref) | copy-start | bytes 7077892
  77.7 0.9 copy-start.7
  78.6 27.6 %copy-start.12 = (f32[128]{0:T(128)S(1)}, f32[128]{0:T(128)}, u32[]{:S(2)}) copy-start(f32[128]{0:T(128)} %param.18) | copy-start | bytes 1540
  78.6 27.7 %copy-start.13 = (f32[128]{0:T(128)S(1)}, f32[128]{0:T(128)}, u32[]{:S(2)}) copy-start(f32[128]{0:T(128)} %param.19) | copy-start | bytes 1540
  94.6 0.7 copy-start.10
  106.3 1.9 %copy-start.1 = (f32[768,1024]{1,0:T(8,128)S(1)}, f32[768,1024]{1,0:T(8,128)}, u32[]{:S(2)}) copy-start(f32[768,1024]{1,0:T(8,128)} %get-tuple-element.31) | copy-start | bytes 9437188
